TPU v7x, 32 devices: a whole 2x2x4 slice. The times are simulated.
32 devices in a mesh: group: 2 (over y), tok: 4 (over z), head: 2 (over x), sub: 2 (over core).
Axes of the slice: x: 2, y: 2, z: 4, core: 2. Of those that a mesh axis runs over, the one named last changes fastest.
Arguments:
- hidden_in: bfloat16 [4096, 4096], P(('group', 'tok')), parts along dimension 0, may hold values from -6 to 6
- norm_gain: bfloat16 [4096], replicated, may hold values from 0.099609375 to 1.8984375
- q_weight: bfloat16 [4096, 1024], P('tok', ('head', 'sub'))
- kv_weight: bfloat16 [4096, 512], P('tok', ('head', 'sub')), may hold values from -0.09375 to 0.09375
- o_weight: bfloat16 [1024, 4096], P(('head', 'sub'), 'tok'), may hold values from -0.25 to 0.25
- doc_lengths: int32 [8], P('group'), parts along dimension 0, may hold values from 1 to 1024, 2048 in all
- task_server: int32 [32, 8], P('group'), parts along dimension 0, may hold values from 0 to 7, as said below
Outputs:
- layer_out: bfloat16 [4096, 4096], P(('group', 'tok'), ('head', 'sub')), parts along dimension 0
- task_lse: float32 [16, 8, 2, 128], P(('group', 'tok', 'sub'), None, 'head'), parts along dimension 0
There are 2 independent parts, one for each index of `group`. A program takes and returns all parts, laid end to end along the dimension named above; an argument that names none is the same for every part. Nothing has to cross between parts.
Inputs may be any that keep to these rules, and one draw needn't show every extreme that they name: `doc_lengths`: documents are laid end to end from token 0; the lengths sum to 2048 and the longest is 1024. `task_server`: A server is a token device's index among 8.
All inputs are finite; a program needn't handle non-finite values.
Results may differ from a plain program's by a relative error of at most 0.0095.
The roundings to bfloat16 on the way count: a program that leaves them out, or rounds other values in their place, can miss the bound.
Values may be sent and summed in bfloat16 or wider, within the bound.
A program may use at most 64 MiB of HBM per device.

v0:
```python
import jax
import jax.numpy as jnp
from jax import lax
from jax.sharding import PartitionSpec as P

BLOCK = 128


rope_base = 500000.0
norm_eps = 1e-05
masked_score = -1e30


def rotate(values_in, positions):
    head_width = values_in.shape[-1]
    half_width = head_width // 2
    frequencies = rope_base ** (-(jnp.arange(half_width, dtype=jnp.float32) * 2.0 / head_width))
    angles = positions.astype(jnp.float32)[:, None] * frequencies[None, :]
    cosine = jnp.concatenate([jnp.cos(angles), jnp.cos(angles)], axis=-1)[:, None, :]
    sine_part = jnp.concatenate([jnp.sin(angles), jnp.sin(angles)], axis=-1)[:, None, :]
    turned = jnp.concatenate([-values_in[..., half_width:], values_in[..., :half_width]], axis=-1)
    return values_in * cosine + turned * sine_part


def document_start(positions, doc_lengths):
    doc_ends = jnp.cumsum(doc_lengths)
    doc_starts = doc_ends - doc_lengths
    inside = doc_starts[None, :] <= positions[:, None]
    return jnp.max(jnp.where(inside, doc_starts[None, :], 0), axis=1)


def attend_groups(queries, query_pos, query_start, key_rows, value_rows, key_base):
    slot_count, block_rows, head_width = queries.shape
    key_block = 4 * block_rows
    scale = head_width ** (-0.5)
    window_len = key_rows.shape[0]

    def one_group(inputs):
        block_queries, block_pos, block_start = inputs
        live_rows = block_pos >= 0
        any_live = jnp.any(live_rows)
        first_key = jnp.min(jnp.where(live_rows, block_start, key_base + window_len)) - key_base
        last_key = jnp.max(jnp.where(live_rows, block_pos, key_base)) - key_base
        lower_block = jnp.where(any_live, first_key // key_block, 0)
        upper_block = jnp.where(any_live, last_key // key_block + 1, 0)

        def advance(block_index, carry):
            running, denominator, numerator = carry
            offset = block_index * key_block
            key_part = lax.dynamic_slice_in_dim(key_rows, offset, key_block, 0)
            value_part = lax.dynamic_slice_in_dim(value_rows, offset, key_block, 0)
            scores = (
                jnp.einsum(
                    "gqd,kd->gqk", block_queries, key_part, preferred_element_type=jnp.float32
                )
                * scale
            )
            key_pos = key_base + offset + jnp.arange(key_block, dtype=jnp.int32)
            allowed = (key_pos[None, None, :] >= block_start[:, :, None]) & (
                key_pos[None, None, :] <= block_pos[:, :, None]
            )
            new_peak = jnp.maximum(
                running, jnp.max(jnp.where(allowed, scores, masked_score), axis=-1)
            )
            weights = jnp.where(allowed, jnp.exp(scores - new_peak[..., None]), 0.0)
            factor = jnp.exp(running - new_peak)
            denominator = denominator * factor + jnp.sum(weights, axis=-1)
            numerator = numerator * factor[..., None] + jnp.einsum(
                "gqk,kd->gqd",
                weights.astype(jnp.bfloat16),
                value_part,
                preferred_element_type=jnp.float32,
            )
            return (new_peak, denominator, numerator)

        start_carry = (
            jnp.full(block_pos.shape, masked_score, jnp.float32),
            jnp.zeros(block_pos.shape, jnp.float32),
            jnp.zeros(block_queries.shape, jnp.float32),
        )
        running, denominator, numerator = lax.fori_loop(
            lower_block, upper_block, advance, start_carry
        )
        safe_total = jnp.where(live_rows, denominator, 1.0)
        result = jnp.where(live_rows[..., None], numerator / safe_total[..., None], 0.0).astype(
            jnp.bfloat16
        )
        spread = jnp.where(live_rows, running + jnp.log(safe_total), 0.0)
        return (result, spread)

    group_count = slot_count // 4
    shaped = (
        queries.reshape(group_count, 4, block_rows, head_width),
        query_pos.reshape(group_count, 4, block_rows),
        query_start.reshape(group_count, 4, block_rows),
    )
    result, spread = lax.map(one_group, shaped)
    return (
        result.reshape(slot_count, block_rows, head_width),
        spread.reshape(slot_count, block_rows),
    )


def body(hidden_in, norm_gain, q_weight, kv_weight, o_weight, doc_lengths, task_server):
    tok_rows = hidden_in.shape[0]
    tok_index = lax.axis_index("tok")
    head_index = lax.axis_index("head")
    sub_index = lax.axis_index("sub")
    my_server = lax.axis_index(("tok", "sub"))
    server_count = lax.axis_size(("tok", "sub"))
    tok_count = lax.axis_size("tok")
    sub_count = lax.axis_size("sub")
    head_dim = kv_weight.shape[1]
    heads_here = q_weight.shape[1] // head_dim
    blocks_here = tok_rows // BLOCK
    tasks_here = blocks_here * heads_here
    group_heads = heads_here * sub_count
    hidden_float = hidden_in.astype(jnp.float32)
    mean_square = jnp.mean(hidden_float * hidden_float, axis=-1, keepdims=True)
    normed = (
        hidden_float * lax.rsqrt(mean_square + norm_eps) * norm_gain.astype(jnp.float32)
    ).astype(jnp.bfloat16)
    q_sum = jnp.dot(
        normed,
        lax.all_gather(q_weight, "tok", axis=0, tiled=True),
        preferred_element_type=jnp.float32,
    )
    kv_sum = jnp.dot(
        normed,
        lax.all_gather(kv_weight, "tok", axis=0, tiled=True),
        preferred_element_type=jnp.float32,
    )
    token_pos = tok_index * tok_rows + jnp.arange(tok_rows, dtype=jnp.int32)
    token_start = document_start(token_pos, doc_lengths)
    relative = token_pos - token_start
    queries = rotate(q_sum.reshape(tok_rows, heads_here, head_dim), relative).astype(jnp.bfloat16)
    rotated_kv = rotate(kv_sum[:, None, :], relative)[:, 0, :]
    kv_part = jnp.where(sub_index == 0, rotated_kv, kv_sum).astype(jnp.bfloat16)
    task_q = (
        queries.reshape(blocks_here, BLOCK, heads_here, head_dim)
        .transpose(0, 2, 1, 3)
        .reshape(tasks_here, BLOCK, head_dim)
    )
    head_table = lax.dynamic_slice_in_dim(task_server, head_index * group_heads, group_heads, 1)
    own_table = lax.dynamic_slice(
        head_table, (tok_index * blocks_here, sub_index * heads_here), (blocks_here, heads_here)
    ).reshape(tasks_here)
    routing = own_table[None, :] == jnp.arange(server_count, dtype=jnp.int32)[:, None]
    outgoing = jnp.einsum(
        "ik,kbd->ibd", routing.astype(jnp.bfloat16), task_q, preferred_element_type=jnp.float32
    ).astype(jnp.bfloat16)
    arrived = lax.all_to_all(outgoing, ("tok", "sub"), split_axis=0, concat_axis=0, tiled=True)
    gathered = lax.all_gather(kv_part, ("tok", "sub"), axis=0, tiled=True).reshape(
        tok_count, sub_count, tok_rows, head_dim
    )
    all_keys = gathered[:, 0].reshape(tok_count * tok_rows, head_dim)
    all_values = gathered[:, 1].reshape(tok_count * tok_rows, head_dim)
    sources = (
        head_table.reshape(tok_count, blocks_here, sub_count, heads_here)
        .transpose(0, 2, 1, 3)
        .reshape(server_count, tasks_here)
    )
    matches = sources == my_server
    slot_live = jnp.any(matches, axis=1)
    block_of_task = jnp.arange(tasks_here, dtype=jnp.int32) // heads_here
    slot_block = jnp.arange(server_count, dtype=jnp.int32) // sub_count * blocks_here + jnp.sum(
        jnp.where(matches, block_of_task[None, :], 0), axis=1
    )
    slot_pos = slot_block[:, None] * BLOCK + jnp.arange(BLOCK, dtype=jnp.int32)[None, :]
    slot_start = document_start(slot_pos.reshape(-1), doc_lengths).reshape(server_count, BLOCK)
    slot_pos = jnp.where(slot_live[:, None], slot_pos, -1)
    results, lse_slots = attend_groups(arrived, slot_pos, slot_start, all_keys, all_values, 0)
    returned = lax.all_to_all(results, ("tok", "sub"), split_axis=0, concat_axis=0, tiled=True)
    own_out = jnp.einsum(
        "ik,ibd->kbd", routing.astype(jnp.bfloat16), returned, preferred_element_type=jnp.float32
    ).astype(jnp.bfloat16)
    attention = (
        own_out.reshape(blocks_here, heads_here, BLOCK, head_dim)
        .transpose(0, 2, 1, 3)
        .reshape(tok_rows, heads_here * head_dim)
    )
    partial_sums = jnp.dot(
        attention,
        lax.all_gather(o_weight, "tok", axis=1, tiled=True),
        preferred_element_type=jnp.float32,
    )
    summed = lax.psum_scatter(
        partial_sums.astype(jnp.bfloat16), ("head", "sub"), scatter_dimension=1, tiled=True
    ).astype(jnp.float32)
    share_cols = summed.shape[1]
    residual = lax.dynamic_slice_in_dim(
        hidden_float, lax.axis_index(("head", "sub")) * share_cols, share_cols, 1
    )
    layer_out = (residual + summed).astype(jnp.bfloat16)
    return (layer_out, lse_slots.reshape(1, server_count, 1, BLOCK))


def solution(mesh):
    placed = (
        P(("group", "tok"), None),
        P(),
        P("tok", ("head", "sub")),
        P("tok", ("head", "sub")),
        P(("head", "sub"), "tok"),
        P("group"),
        P("group", None),
    )
    return jax.shard_map(
        body,
        mesh=mesh,
        in_specs=placed,
        out_specs=(
            P(("group", "tok"), ("head", "sub")),
            P(("group", "tok", "sub"), None, "head", None),
        ),
        check_vma=False,
    )
```

profile of v0, /device:TPU:1, one launch (start us, length us, event | category | flops | bytes accessed | tf_op | source)
XLA Modules:
  0.0 223.5 jit_solution(12779798274977398789)
XLA Ops:
  7.2 0.7 all-gather.7.cloned.1.call-update
  7.9 0.7 all-gather.5.cloned.1.call-update
  8.7 0.8 reduce-window.9
  9.5 0.7 convert_element_type.55
  10.3 0.7 bitcast_subtract_fusion.1
  11.0 3.1 %multiply_reduce_fusion = f32[512]{0:T(512)S(1)} fusion(bf16[512,4096]{1,0:T(8,128)(2,1)} %param.11), kind=kLoop, calls=%fused_computation.34 | loop fusion | flops 6290944 | bytes 4196352 | tf_op jit(solution)/shard_map/reduce_sum | solution.py:119
  14.1 0.5 multiply_sine_fusion
  14.7 24.8 %all-gather.7.cloned.1.call-done = bf16[4096,128]{1,0:T(8,128)(2,1)} async-done(((bf16[1024,128]{1,0:T(8,128)(2,1)}), bf16[4096,128]{1,0:T(8,128)(2,1)}) %all-gather.7.cloned.1.call-update) | async-done | bytes 1048592 | tf_op jit(solution)/shard_map/all_gather | solution.py:130
  39.5 4.1 %fusion.16 = f32[512,128]{0,1:T(8,128)S(1)} fusion(bf16[4096,128]{1,0:T(8,128)(2,1)} %all-gather.7.cloned.1.call-done, f32[4096]{0:T(1024)S(1)} %convert_element_type.55, f32[512]{0:T(512)S(1)} %add_rsqrt_fusion, bf16[512,4096]{1,0:T(8,128)(2,1)} %param.11), kind=kOutput, calls=%fused_computation.37 | convolution fusion | flops 545259520 | bytes 5523456 | tf_op jit(solution)/shard_map/dot_general | solution.py:128
  43.6 0.7 fusion.24
  44.4 0.5 all-gather.11.cloned.1.call-update
  45.1 0.2 bitcast_reduce_fusion
  45.2 0.2 select_reduce_fusion.5
  46.2 1.1 multiply_cosine_fusion.1
  47.5 39.2 %all-gather.5.cloned.1.call-done = bf16[4096,256]{1,0:T(8,128)(2,1)} async-done(((bf16[1024,256]{1,0:T(8,128)(2,1)}), bf16[4096,256]{1,0:T(8,128)(2,1)}) %all-gather.5.cloned.1.call-update) | async-done | bytes 2097168 | tf_op jit(solution)/shard_map/all_gather | solution.py:125
  86.7 4.4 %fusion.17 = f32[512,256]{0,1:T(8,128)S(1)} fusion(bf16[4096,256]{1,0:T(8,128)(2,1)} %all-gather.5.cloned.1.call-done, f32[4096]{0:T(1024)S(1)} %convert_element_type.55, f32[512]{0:T(512)S(1)} %add_rsqrt_fusion, bf16[512,4096]{1,0:T(8,128)(2,1)} %param.11), kind=kOutput, calls=%fused_computation.38 | convolution fusion | flops 1082130432 | bytes 6834176 | tf_op jit(solution)/shard_map/dot_general | solution.py:123
  91.1 0.2 reshape.236
  91.5 0.2 fusion.26
  91.8 0.2 copy.43
  92.0 0.3 convolution_convert_fusion.2
  92.3 0.8 copy.45
  93.1 4.0 %all-to-all-start = ((bf16[8,128,128]{2,1,0:T(8,128)(2,1)}), bf16[8,128,128]{2,1,0:T(8,128)(2,1)S(1)}, u32[]{:S(2)}, u32[]{:S(2)}) async-start(bf16[8,128,128]{2,1,0:T(8,128)(2,1)} %copy.45), calls=%async_computation | async-start | bytes 524288 | tf_op jit(solution)/shard_map/all_to_all | solution.py:152
  97.2 17.1 %all-gather.9.cloned.1.call-done = bf16[4096,128]{0,1:T(8,128)(2,1)} async-done(((bf16[512,128]{0,1:T(8,128)(2,1)}), bf16[4096,128]{0,1:T(8,128)(2,1)}) %all-gather.9.cloned.1.call-update) | async-done | bytes 1048592 | tf_op jit(solution)/shard_map/all_gather | solution.py:153
  114.2 1.8 reshape.240
  116.1 1.5 fusion.37
  117.6 0.9 copy.47
  118.4 0.9 copy.46
  119.3 25.2 %while.50 = (s32[]{:T(128)}, bf16[2,4,128,128]{3,2,1,0:T(8,128)(2,1)}, f32[2,4,128]{2,1,0:T(4,128)S(1)}, s32[2,4,128]{2,1,0:T(4,128)S(1)}, s32[2,4,128]{2,1,0:T(...) while((s32[]{:T(128)}, ...), condition=%wide.region_14.15_spmd, body=%wide.region_6.14_spmd.sunk | while | flops 139270688 | bytes 7159196 | solution.py:97
  119.3 0.7 select_reduce_fusion.8
  124.9 0.7 reduce_or.25
  126.9 2.7 %while.51 = (s32[]{:T(128)}, f32[4,128]{1,0:T(4,128)S(1)}, f32[4,128]{1,0:T(4,128)S(1)}, f32[4,128,128]{2,1,0:T(8,128)S(1)}, s32[]{:T(128)}, /*index=5*/s32[4,12...) while((s32[]{:T(128)}, f32[4,128]{1,0:T(4,128)S(1)}, ...), condition=%wide.region_13.13_spmd, body=%wide.region_10.12_spmd.sunk | while | flops 139068928 | bytes 4116671 | solution.py:81
  127.0 0.4 select_reduce_fusion.9
  127.4 0.3 fusion.50
  127.7 0.6 convolution_add_fusion.2
  128.3 0.4 select_reduce_fusion.9
  128.7 0.3 fusion.50
  129.0 0.6 convolution_add_fusion.2
  129.6 0.3 bitcast_dynamic-update-slice_fusion.4
  129.9 0.7 copy-done.1
  130.6 0.7 select_reduce_fusion.8
  136.2 0.7 reduce_or.25
  138.2 5.3 %while.51 = (s32[]{:T(128)}, f32[4,128]{1,0:T(4,128)S(1)}, f32[4,128]{1,0:T(4,128)S(1)}, f32[4,128,128]{2,1,0:T(8,128)S(1)}, s32[]{:T(128)}, /*index=5*/s32[4,12...) while((s32[]{:T(128)}, f32[4,128]{1,0:T(4,128)S(1)}, ...), condition=%wide.region_13.13_spmd, body=%wide.region_10.12_spmd.sunk | while | flops 139068928 | bytes 4116671 | solution.py:81
  138.2 0.4 select_reduce_fusion.9
  138.6 0.3 fusion.50
  138.9 0.6 convolution_add_fusion.2
  139.5 0.4 select_reduce_fusion.9
  139.9 0.3 fusion.50
  140.3 0.6 convolution_add_fusion.2
  140.9 0.4 select_reduce_fusion.9
  141.3 0.3 fusion.50
  141.6 0.6 convolution_add_fusion.2
  142.2 0.4 select_reduce_fusion.9
  142.6 0.3 fusion.50
  142.9 0.6 convolution_add_fusion.2
  143.5 0.3 bitcast_dynamic-update-slice_fusion.4
  143.8 0.7 copy-done.1
  144.5 19.8 %all_to_all.10 = bf16[8,128,128]{2,1,0:T(8,128)(2,1)S(1)} all-to-all(bf16[8,128,128]{2,1,0:T(8,128)(2,1)} %bitcast.96), channel_id=1, replica_groups=mesh['group'=2,'tok'=4,'head'=2,'sub'=2] {'tok','sub'}, dimensions={0} | all-to-all | bytes 524288 | tf_op jit(solution)/shard_map/all_to_all | solution.py:173
  164.3 0.3 convolution_convert_fusion.1
  164.6 0.2 copy.49
  164.8 0.5 all-gather.11.cloned.1.call-done
  165.3 4.8 %convolution_convert_fusion = bf16[512,4096]{1,0:T(8,128)(2,1)} fusion(bf16[256,4096]{1,0:T(8,128)(2,1)} %all-gather.11.cloned.1.call-done, bf16[64,8,2,128]{3,2,1,0:T(2,128)(2,1)S(1)} %bitcast.91), kind=kOutput, calls=%fused_computation.35 | convolution fusion | flops 1075838976 | bytes 6553600 | tf_op jit(solution)/shard_map/dot_general | solution.py:182
  170.2 7.2 %convert_element_type.54 = f32[512,4096]{1,0:T(8,128)} convert(bf16[512,4096]{1,0:T(8,128)(2,1)} %param.11) | non-fusion elementwise | flops 2097152 | bytes 12582912 | tf_op jit(solution)/shard_map/convert_element_type | solution.py:118
  177.4 36.3 %reduce-scatter.2.cloned.1.call-done = bf16[512,1024]{1,0:T(8,128)(2,1)} async-done(((bf16[512,4096]{1,0:T(8,128)(2,1)}), bf16[512,1024]{1,0:T(8,128)(2,1)}) %reduce-scatter.2.cloned.1.call-update) | async-done | bytes 1048592 | tf_op jit(solution)/shard_map/reduce_scatter | solution.py:187
  213.7 3.2 %add_convert_fusion = bf16[512,1024]{1,0:T(8,128)(2,1)} fusion(bf16[512,1024]{1,0:T(8,128)(2,1)} %reduce-scatter.2.cloned.1.call-done, f32[512,4096]{1,0:T(8,128)} %convert_element_type.54, s32[]{:T(128)S(6)} %select_n.143), kind=kLoop, calls=%fused_computation.36 | loop fusion | flops 1572864 | bytes 4194308 | tf_op jit(solution)/shard_map/convert_element_type | solution.py:194
  (83 shorter events, 2.0 us)
Async XLA Ops:
  7.2 32.3 %all-gather.7.cloned.1.call-start = ((), (), s32[]{:S(2)}) async-start(), calls=%async_computation.4 | async-start | bytes 1310720 | tf_op jit(solution)/shard_map/all_gather | solution.py:130
  7.9 78.8 %all-gather.5.cloned.1.call-start = ((), (), s32[]{:S(2)}) async-start(), calls=%async_computation.3 | async-start | bytes 2621440 | tf_op jit(solution)/shard_map/all_gather | solution.py:125
  8.6 105.6 %all-gather.9.cloned.1.call-start = ((), (), s32[]{:S(2)}) async-start(), calls=%async_computation.5 | async-start | bytes 1179648 | tf_op jit(solution)/shard_map/all_gather | solution.py:153
  14.6 30.3 %copy-start.2 = (s32[16,8]{0,1:T(8,128)S(1)}, s32[16,8]{0,1:T(8,128)}, u32[]{:S(2)}) copy-start(s32[16,8]{0,1:T(8,128)} %param.17) | copy-start | bytes 1540
  44.3 121.0 %all-gather.11.cloned.1.call-start = ((), (), s32[]{:S(2)}) async-start(), calls=%async_computation.6 | async-start | bytes 2621440 | tf_op jit(solution)/shard_map/all_gather | solution.py:184
  93.1 26.2 %all-to-all-start = ((bf16[8,128,128]{2,1,0:T(8,128)(2,1)}), bf16[8,128,128]{2,1,0:T(8,128)(2,1)S(1)}, u32[]{:S(2)}, u32[]{:S(2)}) async-start(bf16[8,128,128]{2,1,0:T(8,128)(2,1)} %copy.45), calls=%async_computation | async-start | bytes 524288 | tf_op jit(solution)/shard_map/all_to_all | solution.py:152
  97.1 116.7 %reduce-scatter.2.cloned.1.call-start = ((), (), s32[]{:S(2)}) async-start(), calls=%async_computation.7 | async-start | bytes 5242880 | tf_op jit(solution)/shard_map/reduce_scatter | solution.py:187
  126.9 2.7 %copy-start = (bf16[2,4,128,128]{3,2,1,0:T(8,128)(2,1)S(1)}, bf16[2,4,128,128]{3,2,1,0:T(8,128)(2,1)}, u32[]{:S(2)}) copy-start(bf16[2,4,128,128]{3,2,1,0:T(8,128)(2,1)} %get-tuple-element.477) | copy-start | bytes 786436 | tf_op jit(solution)/shard_map/while
  129.9 0.7 copy-start.1
  138.2 5.4 %copy-start = (bf16[2,4,128,128]{3,2,1,0:T(8,128)(2,1)S(1)}, bf16[2,4,128,128]{3,2,1,0:T(8,128)(2,1)}, u32[]{:S(2)}) copy-start(bf16[2,4,128,128]{3,2,1,0:T(8,128)(2,1)} %get-tuple-element.477) | copy-start | bytes 786436 | tf_op jit(solution)/shard_map/while
  143.8 0.7 copy-start.1
  144.5 25.7 %copy-start.3 = (f32[2,4,128]{2,1,0:T(4,128)}, f32[2,4,128]{2,1,0:T(4,128)S(1)}, u32[]{:S(2)}) copy-start(f32[2,4,128]{2,1,0:T(4,128)S(1)} %get-tuple-element.185) | copy-start | bytes 12292
Sparse Core Ops, SparseCore 0:
  9.6 29.8 all-gather.6
  41.0 45.5 all-gather.4
  88.3 25.9 all-gather.8
  115.7 49.6 all-gather.10
  170.3 43.4 reduce-scatter.1
where the time goes:
time: 225 us; the launch traced here: 223 us
  waiting for transfers between devices  120 us (53%)
  other arithmetic  24.4 us (11%)
  blocking collectives  19.8 us (9%)
  matrix products  19.6 us (9%)
  between operations  14 us (6%)
  loops' own time  12.8 us (6%)
  local copies, waits for them, and re-layouts  8.86 us (4%)
  starting transfers between devices  4.15 us (2%)
    all_gather x1, waiting for transfers between devices, body(): lax.all_gather(q_weight, 'tok', axis=0, tiled=True)  39.2 us
    reduce_scatter x1, waiting for transfers between devices, body(): lax.psum_scatter(partial_sums.astype(jnp.bfloat16), ('head', 'sub'), scat...  36.3 us
    all_gather x1, waiting for transfers between devices, body(): lax.all_gather(kv_weight, 'tok', axis=0, tiled=True)  24.8 us
    all_to_all x1, blocking collectives, body(): lax.all_to_all(results, ('tok', 'sub'), split_axis=0, concat_axis=0, tile...  19.8 us
    all_gather x1, waiting for transfers between devices, body(): lax.all_gather(kv_part, ('tok', 'sub'), axis=0, tiled=True)  17.1 us
    another operation x1, loops' own time, attend_groups(): result, spread = lax.map(one_group, shaped)  12.5 us
    convert_element_type x1, other arithmetic, body(): hidden_float = hidden_in.astype(jnp.float32)  7.23 us
    dot_general x1, matrix products, body(): jnp.dot(attention, lax.all_gather(o_weight, 'tok', axis=1, tiled=True), p...  4.83 us
  transfers between devices with their start and end apart: 6, of which 5 were waited for; matrix products, arithmetic and copies ran while one was open for 19% of the time, Pallas kernels for 0%

commit v1 on v0

v1 whole, which is shorter than its diff:
```python
import functools

import jax
import jax.numpy as jnp
from jax import lax
from jax.experimental import pallas as pl
from jax.experimental.pallas import tpu as pltpu
from jax.sharding import PartitionSpec as P

BLOCK = 128
HEAD = 128
DOCMAX = 1024
rope_base = 500000.0
norm_eps = 1e-05
masked_score = -1e30
MESH = pl.DeviceIdType.MESH


def kernel(
    sizes,
    doc_ref,
    table_ref,
    hid_ref,
    gain_ref,
    freq_ref,
    q_ref,
    kv_ref,
    o_ref,
    out_ref,
    lse_ref,
    hid,
    normed,
    qw,
    kvw,
    o_stage,
    wo,
    q_acc,
    kv_acc,
    cos_buf,
    sin_buf,
    queries,
    window,
    att,
    lse_mine,
    lse_all,
    loc_sem,
    z_send,
    z_recv,
    y_send,
    y_recv,
    o_send,
    o_recv,
    k_send,
    k_recv,
    kc_send,
    kc_recv,
    a_send,
    a_recv,
    ac_send,
    ac_recv,
    l_send,
    l_recv,
):
    groups, toks, heads, subs = sizes
    y = lax.axis_index("group")
    t = lax.axis_index("tok")
    x = lax.axis_index("head")
    c = lax.axis_index("sub")
    rows, width = hid.shape
    depth = q_ref.shape[0]
    half = depth // 2
    o_half = o_ref.shape[0] // 2
    shares = heads * subs
    mine = x * subs + c
    blocks = rows // BLOCK
    heads_here = q_ref.shape[1] // HEAD
    back = DOCMAX // rows
    docs = doc_ref.shape[0]
    tasks = blocks * heads_here
    sent = []

    def at_half(ref, index, size):
        return ref.at[pl.ds(pl.multiple_of(index * size, size), size)]

    def when(cond, fn):
        if cond is True:
            fn()
        else:
            pl.when(cond)(fn)

    def send(cond, src, dst, send_sem, recv_sem, device):
        copy = pltpu.make_async_remote_copy(
            src_ref=src,
            dst_ref=dst,
            send_sem=send_sem,
            recv_sem=recv_sem,
            device_id=device,
            device_id_type=MESH,
        )
        when(cond, copy.start)
        sent.append((cond, copy))

    def arrived(cond, dst, sem):
        when(cond, pltpu.make_async_copy(dst, dst, sem).wait)

    load_hid = pltpu.make_async_copy(hid_ref, hid, loc_sem.at[0])
    load_q = pltpu.make_async_copy(q_ref, qw.at[t], loc_sem.at[1])
    load_kv = pltpu.make_async_copy(kv_ref, kvw.at[t], loc_sem.at[2])
    load_hid.start()
    load_q.start()
    load_kv.start()

    barrier = pltpu.get_barrier_semaphore()
    count = 0
    for dy in range(groups):
        for dx in range(heads):
            for dc in range(subs):
                if dy or dx or dc:
                    pl.semaphore_signal(
                        barrier,
                        inc=1,
                        device_id=(
                            lax.rem(y + dy, groups),
                            t,
                            lax.rem(x + dx, heads),
                            lax.rem(c + dc, subs),
                        ),
                        device_id_type=MESH,
                    )
                    count += 1
    for dt in range(1, toks):
        for dc in range(subs):
            pl.semaphore_signal(
                barrier,
                inc=1,
                device_id=(y, lax.rem(t + dt, toks), x, lax.rem(c + dc, subs)),
                device_id_type=MESH,
            )
            count += 1
    pl.semaphore_wait(barrier, count)

    slots = (qw, kvw, o_stage)

    def piece(array, shard):
        if array == 2:
            return o_stage.at[shard]
        return at_half(slots[array].at[shard], y, half)

    def pass_on(array, shard, cond, src, direction):
        target = t + (1 if direction == 0 else -1)
        inside = (target < toks) if direction == 0 else (target >= 0)
        send(
            cond & inside,
            src,
            piece(array, shard),
            z_send.at[array, direction, shard],
            z_recv.at[array, shard],
            (y, target, x, c),
        )

    def spread_o(shard, cond, src):
        dest_x, dest_c = shard // subs, lax.rem(shard, subs)
        dst = wo.at[mine, pl.ds(pl.multiple_of(y * o_half, o_half), o_half)]
        for dy in range(groups):
            dest_y = lax.rem(y + dy, groups)
            remote = cond if dy else cond & (shard != mine)
            send(
                remote,
                src,
                dst,
                o_send.at[shard, dy],
                o_recv.at[mine, y],
                (dest_y, t, dest_x, dest_c),
            )
        when(
            cond & (shard == mine),
            pltpu.make_async_copy(src, dst, o_recv.at[mine, y]).start,
        )

    yes = t >= 0
    own = (at_half(q_ref, y, half), at_half(kv_ref, y, half), at_half(o_ref, y, o_half))
    for array in range(2):
        for direction in range(2):
            pass_on(array, t, yes, own[array], direction)
    for direction in range(2):
        pass_on(2, t, yes, own[2], direction)
    spread_o(t, yes, own[2])

    load_hid.wait()
    step_rows = 64

    def norm_rows(step, carry):
        at = pl.ds(pl.multiple_of(step * step_rows, step_rows), step_rows)
        part = hid[at, :].astype(jnp.float32)
        scale = lax.rsqrt(jnp.mean(part * part, axis=-1, keepdims=True) + norm_eps)
        result = (part * scale * gain_ref[...].astype(jnp.float32)).astype(jnp.bfloat16)
        for shard in range(toks):
            for side in range(2):
                first = shard * depth + side * half
                normed[shard, side, at, :] = result[:, first : first + half]
        return carry

    lax.fori_loop(0, rows // step_rows, norm_rows, 0)

    def doc_start(pos):
        start = jnp.zeros_like(pos)
        total = doc_ref[0] * 0
        for doc in range(docs):
            start = jnp.where(total <= pos, total, start)
            total = total + doc_ref[doc]
        return start

    def angles(step, carry):
        at = pl.ds(pl.multiple_of(step * BLOCK, BLOCK), BLOCK)
        pos = t * rows + step * BLOCK + lax.broadcasted_iota(jnp.int32, (BLOCK, HEAD), 0)
        angle = (pos - doc_start(pos)).astype(jnp.float32) * freq_ref[...]
        cos_buf[at, :] = jnp.cos(angle)
        sign = jnp.where(lax.broadcasted_iota(jnp.int32, (BLOCK, HEAD), 1) < HEAD // 2, -1.0, 1.0)
        sin_buf[at, :] = jnp.sin(angle) * sign
        return carry

    lax.fori_loop(0, blocks, angles, 0)

    def project(shard, side, first=False):
        at = pl.ds(pl.multiple_of(side * half, half), half)
        part = normed[shard, side]
        q_part = jnp.dot(part, qw[shard, at, :], preferred_element_type=jnp.float32)
        kv_part = jnp.dot(part, kvw[shard, at, :], preferred_element_type=jnp.float32)
        if first:
            q_acc[...] = q_part
            kv_acc[...] = kv_part
        else:
            q_acc[...] += q_part
            kv_acc[...] += kv_part

    load_q.wait()
    load_kv.wait()
    project(t, 0, first=True)
    project(t, 1)

    other = lax.rem(y + 1, groups)
    for k in range(1, toks):
        for direction in range(2):
            shard = t - k if direction == 0 else t + k
            valid = (shard >= 0) if direction == 0 else (shard < toks)
            for array in range(2):
                arrived(valid, piece(array, shard), z_recv.at[array, shard])
                pass_on(array, shard, valid, piece(array, shard), direction)
                send(
                    valid,
                    piece(array, shard),
                    piece(array, shard),
                    y_send.at[array, shard],
                    y_recv.at[array, shard],
                    (other, t, x, c),
                )
        for direction in range(2):
            shard = t - k if direction == 0 else t + k
            valid = (shard >= 0) if direction == 0 else (shard < toks)
            pl.when(valid)(functools.partial(project, shard, y))
    for k in range(1, toks):
        for direction in range(2):
            shard = t - k if direction == 0 else t + k
            valid = (shard >= 0) if direction == 0 else (shard < toks)
            arrived(valid, o_stage.at[shard], z_recv.at[2, shard])
            pass_on(2, shard, valid, o_stage.at[shard], direction)
            spread_o(shard, valid, o_stage.at[shard])
            for array in range(2):
                arrived(
                    valid, at_half(slots[array].at[shard], other, half), y_recv.at[array, shard]
                )
            pl.when(valid)(functools.partial(project, shard, other))

    def rotated(u):
        return u * cos_buf[...] + pltpu.roll(u, HEAD // 2, 1) * sin_buf[...]

    kv_raw = kv_acc[...]
    own_rows = pl.ds(back * rows, rows)
    window[c, own_rows, :] = jnp.where(c == 0, rotated(kv_raw), kv_raw).astype(jnp.bfloat16)
    twin = lax.rem(c + 1, subs)
    for j in range(1, back + 1):
        send(
            t + j < toks,
            window.at[c, own_rows],
            window.at[c, pl.ds((back - j) * rows, rows)],
            k_send.at[j - 1],
            k_recv.at[j - 1],
            (y, t + j, x, c),
        )
    send(
        True,
        window.at[c, own_rows],
        window.at[c, own_rows],
        kc_send.at[0],
        kc_recv.at[0],
        (y, t, x, twin),
    )
    for h in range(heads_here):
        turned = rotated(q_acc[:, h * HEAD : (h + 1) * HEAD]).astype(jnp.bfloat16)
        for b in range(blocks):
            queries[b, h * BLOCK : (h + 1) * BLOCK, :] = turned[b * BLOCK : (b + 1) * BLOCK]
    for j in range(1, back + 1):
        at = pl.ds((back - j) * rows, rows)

        def blank(at=at):
            window[:, at, :] = jnp.zeros((2, rows, HEAD), jnp.bfloat16)

        pl.when(t < j)(blank)
        arrived(t >= j, window.at[c, at], k_recv.at[j - 1])
        send(
            t >= j,
            window.at[c, at],
            window.at[c, at],
            kc_send.at[j],
            kc_recv.at[j],
            (y, t, x, twin),
        )
    arrived(True, window.at[twin, own_rows], kc_recv.at[0])
    for j in range(1, back + 1):
        at = pl.ds((back - j) * rows, rows)
        arrived(t >= j, window.at[twin, at], kc_recv.at[j])

    reach = DOCMAX + BLOCK
    stack = heads_here * BLOCK
    scale = HEAD ** (-0.5)
    diagonal = lax.broadcasted_iota(jnp.int32, (BLOCK, BLOCK), 0) == lax.broadcasted_iota(
        jnp.int32, (BLOCK, BLOCK), 1
    )
    for b in range(blocks):
        keys = window[0, b * BLOCK : b * BLOCK + reach, :]
        values = window[1, b * BLOCK : b * BLOCK + reach, :]
        scores = (
            lax.dot_general(
                queries[b], keys, (((1,), (1,)), ((), ())), preferred_element_type=jnp.float32
            )
            * scale
        )
        row = lax.broadcasted_iota(jnp.int32, (stack, 1), 0)
        pos = t * rows + b * BLOCK + lax.rem(row, BLOCK)
        start = doc_start(pos)
        key_pos = (t - back) * rows + b * BLOCK + lax.broadcasted_iota(jnp.int32, (1, reach), 1)
        allowed = (key_pos >= start) & (key_pos <= pos)
        scores = jnp.where(allowed, scores, masked_score)
        peak = jnp.max(scores, axis=-1, keepdims=True)
        weights = jnp.exp(scores - peak)
        denom = jnp.sum(weights, axis=-1, keepdims=True)
        mixed = jnp.dot(weights.astype(jnp.bfloat16), values, preferred_element_type=jnp.float32)
        mixed = (mixed / denom).astype(jnp.bfloat16)
        spread = peak + jnp.log(denom)
        for h in range(heads_here):
            att[mine, b, :, h * HEAD : (h + 1) * HEAD] = mixed[h * BLOCK : (h + 1) * BLOCK]
            lse_mine[pl.ds(b * heads_here + h, 1), :] = jnp.sum(
                jnp.where(diagonal, spread[h * BLOCK : (h + 1) * BLOCK], 0.0),
                axis=0,
                keepdims=True,
            )
        for dx in range(1, heads):
            send(
                True,
                att.at[mine, b],
                att.at[mine, b],
                a_send.at[dx, b],
                a_recv.at[x, b],
                (y, t, lax.rem(x + dx, heads), c),
            )
        send(
            True,
            att.at[mine, b],
            att.at[mine, b],
            ac_send.at[0, b],
            ac_recv.at[x, b],
            (y, t, x, twin),
        )

    me = t * subs + c
    for dt in range(toks):
        for dc in range(subs):
            if dt or dc:
                send(
                    True,
                    lse_mine,
                    lse_all.at[me],
                    l_send.at[dt * subs + dc],
                    l_recv.at[me],
                    (y, lax.rem(t + dt, toks), x, lax.rem(c + dc, subs)),
                )
    lse_all[me] = lse_mine[...]

    for r in range(shares):
        for side in range(2):
            dst = wo.at[r, pl.ds(side * o_half, o_half)]
            arrived(True, dst, o_recv.at[r, side])
    share_cols = out_ref.shape[1]
    columns = pl.ds(pl.multiple_of(mine * share_cols, share_cols), share_cols)
    for b in range(blocks):
        for dx in range(1, heads):
            source = lax.rem(x + dx, heads)
            arrived(True, att.at[source * subs + c, b], a_recv.at[source, b])
            send(
                True,
                att.at[source * subs + c, b],
                att.at[source * subs + c, b],
                ac_send.at[dx, b],
                ac_recv.at[source, b],
                (y, t, x, twin),
            )
    for b in range(blocks):
        for dx in range(heads):
            source = lax.rem(x + dx, heads)
            arrived(True, att.at[source * subs + twin, b], ac_recv.at[source, b])
        at = slice(b * BLOCK, (b + 1) * BLOCK)
        summed = jnp.zeros((BLOCK, share_cols), jnp.float32)
        for r in range(shares):
            summed += (
                jnp.dot(att[r, b], wo[r], preferred_element_type=jnp.float32)
                .astype(jnp.bfloat16)
                .astype(jnp.float32)
            )
        out_ref[at, :] = (hid[at, columns].astype(jnp.float32) + summed).astype(jnp.bfloat16)

    group_heads = heads_here * subs
    for dt in range(toks):
        for dc in range(subs):
            source = lax.rem(t + dt, toks) * subs + lax.rem(c + dc, subs)
            if dt or dc:
                arrived(True, lse_all.at[source], l_recv.at[source])
    for source in range(toks * subs):
        kept = jnp.zeros((1, BLOCK), jnp.float32)
        for task in range(tasks):
            server = table_ref[
                (source // subs) * blocks + task // heads_here,
                x * group_heads + (source % subs) * heads_here + task % heads_here,
            ]
            kept = kept + jnp.where(server == me, lse_all[source, task : task + 1, :], 0.0)
        lse_ref[source : source + 1, :] = kept

    for cond, copy in sent:
        when(cond, copy.wait_send)


def body(sizes, hidden_in, norm_gain, q_weight, kv_weight, o_weight, doc_lengths, task_server):
    groups, toks, heads, subs = sizes
    rows, width = hidden_in.shape
    depth, q_cols = q_weight.shape
    o_rows, o_cols = o_weight.shape
    shares = heads * subs
    assert groups == 2 and subs == 2 and toks == shares
    assert width // shares == o_cols and DOCMAX % rows == 0
    blocks = rows // BLOCK
    heads_here = q_cols // HEAD
    back = DOCMAX // rows
    tasks = blocks * heads_here
    servers = toks * subs
    half = jnp.arange(HEAD // 2, dtype=jnp.float32)
    freq = rope_base ** (-(half * 2.0 / HEAD))
    freq = jnp.concatenate([freq, freq])[None, :]
    bf16, f32 = jnp.bfloat16, jnp.float32
    dma = pltpu.SemaphoreType.DMA
    any_spec = pl.BlockSpec(memory_space=pl.ANY)
    vmem = pl.BlockSpec(memory_space=pltpu.VMEM)
    smem = pl.BlockSpec(memory_space=pltpu.SMEM)
    layer_out, lse = pl.pallas_call(
        functools.partial(kernel, sizes),
        out_shape=(
            jax.ShapeDtypeStruct((rows, o_cols), bf16),
            jax.ShapeDtypeStruct((servers, BLOCK), f32),
        ),
        in_specs=[smem, smem, any_spec, vmem, vmem, any_spec, any_spec, any_spec],
        out_specs=(vmem, vmem),
        scratch_shapes=[
            pltpu.VMEM((rows, width), bf16),
            pltpu.VMEM((toks, 2, rows, depth // 2), bf16),
            pltpu.VMEM((toks, depth, q_cols), bf16),
            pltpu.VMEM((toks, depth, HEAD), bf16),
            pltpu.VMEM((toks, o_rows // 2, o_cols), bf16),
            pltpu.VMEM((shares, o_rows, o_cols), bf16),
            pltpu.VMEM((rows, q_cols), f32),
            pltpu.VMEM((rows, HEAD), f32),
            pltpu.VMEM((rows, HEAD), f32),
            pltpu.VMEM((rows, HEAD), f32),
            pltpu.VMEM((blocks, heads_here * BLOCK, HEAD), bf16),
            pltpu.VMEM((2, (back + 1) * rows, HEAD), bf16),
            pltpu.VMEM((shares, blocks, BLOCK, q_cols), bf16),
            pltpu.VMEM((tasks, BLOCK), f32),
            pltpu.VMEM((servers, tasks, BLOCK), f32),
            dma((3,)),
            dma((3, 2, toks)),
            dma((3, toks)),
            dma((2, toks)),
            dma((2, toks)),
            dma((toks, groups)),
            dma((shares, 2)),
            dma((back,)),
            dma((back,)),
            dma((back + 1,)),
            dma((back + 1,)),
            dma((heads, blocks)),
            dma((heads, blocks)),
            dma((heads, blocks)),
            dma((heads, blocks)),
            dma((servers,)),
            dma((servers,)),
        ],
        compiler_params=pltpu.CompilerParams(
            collective_id=0, has_side_effects=True, vmem_limit_bytes=56 * 1024 * 1024
        ),
        cost_estimate=pl.CostEstimate(
            flops=4 * 10**9, bytes_accessed=8 * 2**20, transcendentals=2 * 10**6
        ),
    )(
        doc_lengths,
        task_server,
        hidden_in,
        norm_gain[None, :],
        freq,
        q_weight,
        kv_weight,
        o_weight,
    )
    return (layer_out, lse.reshape(1, servers, 1, BLOCK))


def solution(mesh):
    placed = (
        P(("group", "tok"), None),
        P(),
        P("tok", ("head", "sub")),
        P("tok", ("head", "sub")),
        P(("head", "sub"), "tok"),
        P("group"),
        P("group", None),
    )
    sizes = tuple(mesh.shape[name] for name in ("group", "tok", "head", "sub"))
    return jax.shard_map(
        functools.partial(body, sizes),
        mesh=mesh,
        in_specs=placed,
        out_specs=(
            P(("group", "tok"), ("head", "sub")),
            P(("group", "tok", "sub"), None, "head", None),
        ),
        check_vma=False,
    )
```

time: 225 us -> 84.1 us (0.37)
  the two profiles are of different devices: /device:TPU:1 before, /device:TPU:6 now
where the time goes in v1:
time: 84.1 us; the launch traced here: 83.8 us
  Pallas kernels  76.3 us (91%)
  local copies, waits for them, and re-layouts  6.19 us (7%)
    pallas_call x1, Pallas kernels, body(): pl.pallas_call(functools.partial(kernel, sizes), out_shape=(jax.ShapeDtyp...  76.3 us
    unnamed x3, local copies, waits for them, and re-layouts  4.88 us

profile of v1, /device:TPU:6, one launch (start us, length us, event | category | flops | bytes accessed | tf_op | source)
XLA Modules:
  0.0 83.8 jit_solution(5442242169357225540)
XLA Ops:
  0.6 0.6 maximum_bitcast_fusion.freq_ref
  1.2 1.4 %copy.9.table_ref = s32[16,8]{1,0:T(8,128)} copy(s32[16,8]{0,1:T(8,128)} %param.13) | data formatting | bytes 1024 | tf_op args[6]
  2.6 1.3 %broadcast_in_dim.6.gain_ref = bf16[1,4096]{1,0:T(2,128)(2,1)} reshape(bf16[4096]{0:T(1024)(128)(2,1)} %param.8) | data formatting | bytes 16384 | tf_op jit(solution)/shard_map/broadcast_in_dim | solution.py:514
  3.9 76.3 %shard_map.86 = (bf16[512,1024]{1,0:T(8,128)(2,1)}, f32[8,128]{1,0:T(8,128)}) custom-call(s32[4]{0:T(128)} %doc_ref.1, s32[16,8]{1,0:T(8,128)} %copy.9.table_ref, bf16[512,4096]{1,0:T(8,128)(2,1)} %hid_ref.1, bf16[1,4096]{1,0:T(2,128)(2,1)} %broadcast_in_dim.6.gain_ref, f32[1,128]{1,0:T(1,128)} %maximum_bitcast_fusion.freq_ref, bf16[1024,256]{1,0:T(8,128)(2,1)} %q_ref.1, ...), custom_call_target="tpu_custom_call" | custom-call | flops 4000000000 | bytes 8388608 | tf_op jit(solution)/shard_map/pallas_call | solution.py:462
  80.2 2.3 %copy.13 = bf16[512,1024]{1,0:T(8,128)(2,1)} copy(bf16[512,1024]{1,0:T(8,128)(2,1)} %get-tuple-element.10) | data formatting | bytes 2097152
  82.5 1.3 %copy.14 = f32[1,8,1,128]{3,2,1,0:T(1,128)} copy(f32[1,8,1,128]{3,2,1,0:T(1,128)} %bitcast.5) | data formatting | bytes 8192
  (1 shorter events, 0.0 us)

commit v2 on v1

--- a/solution.py
+++ b/solution.py
@@ -182,9 +182,6 @@
     for array in range(2):
         for direction in range(2):
             pass_on(array, t, yes, own[array], direction)
-    for direction in range(2):
-        pass_on(2, t, yes, own[2], direction)
-    spread_o(t, yes, own[2])
 
     load_hid.wait()
     step_rows = 64
@@ -219,7 +216,6 @@
         sin_buf[at, :] = jnp.sin(angle) * sign
         return carry
 
-    lax.fori_loop(0, blocks, angles, 0)
 
     def project(shard, side, first=False):
         at = pl.ds(pl.multiple_of(side * half, half), half)
@@ -233,16 +229,31 @@
             q_acc[...] += q_part
             kv_acc[...] += kv_part
 
-    load_q.wait()
-    load_kv.wait()
-    project(t, 0, first=True)
-    project(t, 1)
-
     other = lax.rem(y + 1, groups)
+
+    def from_step(k, direction):
+        shard = t - k if direction == 0 else t + k
+        return shard, (shard >= 0) if direction == 0 else (shard < toks)
+
+    def other_halves(k):
+        for direction in range(2):
+            shard, valid = from_step(k, direction)
+            for array in range(2):
+                arrived(
+                    valid, at_half(slots[array].at[shard], other, half), y_recv.at[array, shard]
+                )
+            pl.when(valid)(functools.partial(project, shard, other))
+
+    def chain_o(k):
+        for direction in range(2):
+            shard, valid = from_step(k, direction)
+            arrived(valid, o_stage.at[shard], z_recv.at[2, shard])
+            pass_on(2, shard, valid, o_stage.at[shard], direction)
+            spread_o(shard, valid, o_stage.at[shard])
+
     for k in range(1, toks):
         for direction in range(2):
-            shard = t - k if direction == 0 else t + k
-            valid = (shard >= 0) if direction == 0 else (shard < toks)
+            shard, valid = from_step(k, direction)
             for array in range(2):
                 arrived(valid, piece(array, shard), z_recv.at[array, shard])
                 pass_on(array, shard, valid, piece(array, shard), direction)
@@ -254,22 +265,22 @@
                     y_recv.at[array, shard],
                     (other, t, x, c),
                 )
+        if k == max(toks - 2, 1):
+            for direction in range(2):
+                pass_on(2, t, yes, own[2], direction)
+            spread_o(t, yes, own[2])
+        if k == 1:
+            lax.fori_loop(0, blocks, angles, 0)
+            load_q.wait()
+            load_kv.wait()
+            project(t, 0, first=True)
+            project(t, 1)
+        else:
+            other_halves(k - 1)
         for direction in range(2):
-            shard = t - k if direction == 0 else t + k
-            valid = (shard >= 0) if direction == 0 else (shard < toks)
+            shard, valid = from_step(k, direction)
             pl.when(valid)(functools.partial(project, shard, y))
-    for k in range(1, toks):
-        for direction in range(2):
-            shard = t - k if direction == 0 else t + k
-            valid = (shard >= 0) if direction == 0 else (shard < toks)
-            arrived(valid, o_stage.at[shard], z_recv.at[2, shard])
-            pass_on(2, shard, valid, o_stage.at[shard], direction)
-            spread_o(shard, valid, o_stage.at[shard])
-            for array in range(2):
-                arrived(
-                    valid, at_half(slots[array].at[shard], other, half), y_recv.at[array, shard]
-                )
-            pl.when(valid)(functools.partial(project, shard, other))
+    other_halves(toks - 1)
 
     def rotated(u):
         return u * cos_buf[...] + pltpu.roll(u, HEAD // 2, 1) * sin_buf[...]
@@ -299,6 +310,7 @@
         turned = rotated(q_acc[:, h * HEAD : (h + 1) * HEAD]).astype(jnp.bfloat16)
         for b in range(blocks):
             queries[b, h * BLOCK : (h + 1) * BLOCK, :] = turned[b * BLOCK : (b + 1) * BLOCK]
+    chain_o(1)
     for j in range(1, back + 1):
         at = pl.ds((back - j) * rows, rows)
 
@@ -326,6 +338,19 @@
     diagonal = lax.broadcasted_iota(jnp.int32, (BLOCK, BLOCK), 0) == lax.broadcasted_iota(
         jnp.int32, (BLOCK, BLOCK), 1
     )
+    def forward(b):
+        for dx in range(1, heads):
+            source = lax.rem(x + dx, heads)
+            arrived(True, att.at[source * subs + c, b], a_recv.at[source, b])
+            send(
+                True,
+                att.at[source * subs + c, b],
+                att.at[source * subs + c, b],
+                ac_send.at[dx, b],
+                ac_recv.at[source, b],
+                (y, t, x, twin),
+            )
+
     for b in range(blocks):
         keys = window[0, b * BLOCK : b * BLOCK + reach, :]
         values = window[1, b * BLOCK : b * BLOCK + reach, :]
@@ -371,6 +396,13 @@
             ac_recv.at[x, b],
             (y, t, x, twin),
         )
+        if b == 0 and toks > 2:
+            chain_o(2)
+        if b:
+            forward(b - 1)
+        if b == blocks - 2:
+            for k in range(3, toks):
+                chain_o(k)
 
     me = t * subs + c
     for dt in range(toks):
@@ -392,30 +424,23 @@
             arrived(True, dst, o_recv.at[r, side])
     share_cols = out_ref.shape[1]
     columns = pl.ds(pl.multiple_of(mine * share_cols, share_cols), share_cols)
-    for b in range(blocks):
-        for dx in range(1, heads):
-            source = lax.rem(x + dx, heads)
-            arrived(True, att.at[source * subs + c, b], a_recv.at[source, b])
-            send(
-                True,
-                att.at[source * subs + c, b],
-                att.at[source * subs + c, b],
-                ac_send.at[dx, b],
-                ac_recv.at[source, b],
-                (y, t, x, twin),
-            )
-    for b in range(blocks):
-        for dx in range(heads):
-            source = lax.rem(x + dx, heads)
-            arrived(True, att.at[source * subs + twin, b], ac_recv.at[source, b])
-        at = slice(b * BLOCK, (b + 1) * BLOCK)
-        summed = jnp.zeros((BLOCK, share_cols), jnp.float32)
+    pair = 2
+    for first in range(0, blocks, pair):
+        if first + pair == blocks:
+            forward(blocks - 1)
+        for b in range(first, first + pair):
+            for dx in range(heads):
+                source = lax.rem(x + dx, heads)
+                arrived(True, att.at[source * subs + twin, b], ac_recv.at[source, b])
+        at = slice(first * BLOCK, (first + pair) * BLOCK)
+        summed = jnp.zeros((pair * BLOCK, share_cols), jnp.float32)
         for r in range(shares):
-            summed += (
-                jnp.dot(att[r, b], wo[r], preferred_element_type=jnp.float32)
-                .astype(jnp.bfloat16)
-                .astype(jnp.float32)
-            )
+            product = jnp.dot(
+                att[r, first : first + pair].reshape(pair * BLOCK, att.shape[3]),
+                wo[r],
+                preferred_element_type=jnp.float32,
+            )
+            summed += product.astype(jnp.bfloat16).astype(jnp.float32)
         out_ref[at, :] = (hid[at, columns].astype(jnp.float32) + summed).astype(jnp.bfloat16)
 
     group_heads = heads_here * subs

time: 84.1 us -> 104 us (1.24)
  the two profiles are of different devices: /device:TPU:6 before, /device:TPU:3 now
where the time goes in v2:
time: 104 us
  Pallas kernels  96.1 us (92%)
  local copies, waits for them, and re-layouts  6.19 us (6%)
    pallas_call x1, Pallas kernels, body(): pl.pallas_call(functools.partial(kernel, sizes), out_shape=(jax.ShapeDtyp...  96.1 us
    unnamed x3, local copies, waits for them, and re-layouts  4.88 us

profile of v2, /device:TPU:3, one launch (start us, length us, event | category | flops | bytes accessed | tf_op | source)
XLA Modules:
  0.0 103.5 jit_solution(5600729581071508762)
XLA Ops:
  0.6 0.6 maximum_bitcast_fusion.freq_ref
  1.2 1.4 %copy.9.table_ref = s32[16,8]{1,0:T(8,128)} copy(s32[16,8]{0,1:T(8,128)} %param.13) | data formatting | bytes 1024 | tf_op args[6]
  2.6 1.3 %broadcast_in_dim.6.gain_ref = bf16[1,4096]{1,0:T(2,128)(2,1)} reshape(bf16[4096]{0:T(1024)(128)(2,1)} %param.8) | data formatting | bytes 16384 | tf_op jit(solution)/shard_map/broadcast_in_dim | solution.py:539
  3.9 96.1 %shard_map.86 = (bf16[512,1024]{1,0:T(8,128)(2,1)}, f32[8,128]{1,0:T(8,128)}) custom-call(s32[4]{0:T(128)} %doc_ref.1, s32[16,8]{1,0:T(8,128)} %copy.9.table_ref, bf16[512,4096]{1,0:T(8,128)(2,1)} %hid_ref.1, bf16[1,4096]{1,0:T(2,128)(2,1)} %broadcast_in_dim.6.gain_ref, f32[1,128]{1,0:T(1,128)} %maximum_bitcast_fusion.freq_ref, bf16[1024,256]{1,0:T(8,128)(2,1)} %q_ref.1, ...), custom_call_target="tpu_custom_call" | custom-call | flops 4000000000 | bytes 8388608 | tf_op jit(solution)/shard_map/pallas_call | solution.py:487
  100.0 2.3 %copy.13 = bf16[512,1024]{1,0:T(8,128)(2,1)} copy(bf16[512,1024]{1,0:T(8,128)(2,1)} %get-tuple-element.10) | data formatting | bytes 2097152
  102.2 1.3 %copy.14 = f32[1,8,1,128]{3,2,1,0:T(1,128)} copy(f32[1,8,1,128]{3,2,1,0:T(1,128)} %bitcast.5) | data formatting | bytes 8192
  (1 shorter events, 0.0 us)

commit v3 on v2

--- a/solution.py
+++ b/solution.py
@@ -182,6 +182,7 @@
     for array in range(2):
         for direction in range(2):
             pass_on(array, t, yes, own[array], direction)
+    spread_o(t, yes, own[2])
 
     load_hid.wait()
     step_rows = 64
@@ -265,10 +266,11 @@
                     y_recv.at[array, shard],
                     (other, t, x, c),
                 )
-        if k == max(toks - 2, 1):
+        if k == 1:
             for direction in range(2):
                 pass_on(2, t, yes, own[2], direction)
-            spread_o(t, yes, own[2])
+        else:
+            chain_o(k - 1)
         if k == 1:
             lax.fori_loop(0, blocks, angles, 0)
             load_q.wait()
@@ -310,7 +312,6 @@
         turned = rotated(q_acc[:, h * HEAD : (h + 1) * HEAD]).astype(jnp.bfloat16)
         for b in range(blocks):
             queries[b, h * BLOCK : (h + 1) * BLOCK, :] = turned[b * BLOCK : (b + 1) * BLOCK]
-    chain_o(1)
     for j in range(1, back + 1):
         at = pl.ds((back - j) * rows, rows)
 
@@ -327,6 +328,7 @@
             kc_recv.at[j],
             (y, t, x, twin),
         )
+    chain_o(toks - 1)
     arrived(True, window.at[twin, own_rows], kc_recv.at[0])
     for j in range(1, back + 1):
         at = pl.ds((back - j) * rows, rows)
@@ -396,13 +398,8 @@
             ac_recv.at[x, b],
             (y, t, x, twin),
         )
-        if b == 0 and toks > 2:
-            chain_o(2)
         if b:
             forward(b - 1)
-        if b == blocks - 2:
-            for k in range(3, toks):
-                chain_o(k)
 
     me = t * subs + c
     for dt in range(toks):

time: 104 us -> 90.5 us (0.87)
  the two profiles are of different devices: /device:TPU:3 before, /device:TPU:1 now
where the time goes in v3:
time: 90.5 us; the launch traced here: 90.2 us
  Pallas kernels  82.8 us (91%)
  local copies, waits for them, and re-layouts  6.19 us (7%)
    pallas_call x1, Pallas kernels, body(): pl.pallas_call(functools.partial(kernel, sizes), out_shape=(jax.ShapeDtyp...  82.8 us
    unnamed x3, local copies, waits for them, and re-layouts  4.88 us

profile of v3, /device:TPU:1, one launch (start us, length us, event | category | flops | bytes accessed | tf_op | source)
XLA Modules:
  0.0 90.2 jit_solution(10267621621518509314)
XLA Ops:
  0.6 0.6 maximum_bitcast_fusion.freq_ref
  1.2 1.4 %copy.9.table_ref = s32[16,8]{1,0:T(8,128)} copy(s32[16,8]{0,1:T(8,128)} %param.13) | data formatting | bytes 1024 | tf_op args[6]
  2.6 1.3 %broadcast_in_dim.6.gain_ref = bf16[1,4096]{1,0:T(2,128)(2,1)} reshape(bf16[4096]{0:T(1024)(128)(2,1)} %param.8) | data formatting | bytes 16384 | tf_op jit(solution)/shard_map/broadcast_in_dim | solution.py:536
  3.9 82.8 %shard_map.86 = (bf16[512,1024]{1,0:T(8,128)(2,1)}, f32[8,128]{1,0:T(8,128)}) custom-call(s32[4]{0:T(128)} %doc_ref.1, s32[16,8]{1,0:T(8,128)} %copy.9.table_ref, bf16[512,4096]{1,0:T(8,128)(2,1)} %hid_ref.1, bf16[1,4096]{1,0:T(2,128)(2,1)} %broadcast_in_dim.6.gain_ref, f32[1,128]{1,0:T(1,128)} %maximum_bitcast_fusion.freq_ref, bf16[1024,256]{1,0:T(8,128)(2,1)} %q_ref.1, ...), custom_call_target="tpu_custom_call" | custom-call | flops 4000000000 | bytes 8388608 | tf_op jit(solution)/shard_map/pallas_call | solution.py:484
  86.7 2.3 %copy.13 = bf16[512,1024]{1,0:T(8,128)(2,1)} copy(bf16[512,1024]{1,0:T(8,128)(2,1)} %get-tuple-element.10) | data formatting | bytes 2097152
  88.9 1.3 %copy.14 = f32[1,8,1,128]{3,2,1,0:T(1,128)} copy(f32[1,8,1,128]{3,2,1,0:T(1,128)} %bitcast.5) | data formatting | bytes 8192
  (1 shorter events, 0.0 us)

commit v4 on v3

--- a/solution.py
+++ b/solution.py
@@ -249,7 +249,6 @@
         for direction in range(2):
             shard, valid = from_step(k, direction)
             arrived(valid, o_stage.at[shard], z_recv.at[2, shard])
-            pass_on(2, shard, valid, o_stage.at[shard], direction)
             spread_o(shard, valid, o_stage.at[shard])
 
     for k in range(1, toks):
@@ -267,10 +266,16 @@
                     (other, t, x, c),
                 )
         if k == 1:
-            for direction in range(2):
-                pass_on(2, t, yes, own[2], direction)
-        else:
-            chain_o(k - 1)
+            for j in range(1, toks):
+                for target in (t - j, t + j):
+                    send(
+                        (target >= 0) & (target < toks),
+                        own[2],
+                        o_stage.at[t],
+                        z_send.at[2, 0, target],
+                        z_recv.at[2, t],
+                        (y, target, x, c),
+                    )
         if k == 1:
             lax.fori_loop(0, blocks, angles, 0)
             load_q.wait()
@@ -282,6 +287,7 @@
         for direction in range(2):
             shard, valid = from_step(k, direction)
             pl.when(valid)(functools.partial(project, shard, y))
+    chain_o(1)
     other_halves(toks - 1)
 
     def rotated(u):
@@ -328,7 +334,8 @@
             kc_recv.at[j],
             (y, t, x, twin),
         )
-    chain_o(toks - 1)
+    for k in range(2, toks):
+        chain_o(k)
     arrived(True, window.at[twin, own_rows], kc_recv.at[0])
     for j in range(1, back + 1):
         at = pl.ds((back - j) * rows, rows)

time: 90.5 us -> 102 us (1.13)
  Pallas kernels: 82.8 us -> 93.9 us
    pallas_call x1, Pallas kernels: 82.8 us -> 93.9 us  [body(): pl.pallas_call(functools.partial(kernel, sizes), out_shape=(jax.ShapeDtyp...]
where the time goes in v4:
time: 102 us; the launch traced here: 101 us
  Pallas kernels  93.9 us (92%)
  local copies, waits for them, and re-layouts  6.19 us (6%)
    pallas_call x1, Pallas kernels, body(): pl.pallas_call(functools.partial(kernel, sizes), out_shape=(jax.ShapeDtyp...  93.9 us
    unnamed x3, local copies, waits for them, and re-layouts  4.88 us

profile of v4, /device:TPU:1, one launch (start us, length us, event | category | flops | bytes accessed | tf_op | source)
XLA Modules:
  0.0 101.4 jit_solution(16683099816921255535)
XLA Ops:
  0.6 0.6 maximum_bitcast_fusion.freq_ref
  1.2 1.4 %copy.9.table_ref = s32[16,8]{1,0:T(8,128)} copy(s32[16,8]{0,1:T(8,128)} %param.13) | data formatting | bytes 1024 | tf_op args[6]
  2.6 1.3 %broadcast_in_dim.6.gain_ref = bf16[1,4096]{1,0:T(2,128)(2,1)} reshape(bf16[4096]{0:T(1024)(128)(2,1)} %param.8) | data formatting | bytes 16384 | tf_op jit(solution)/shard_map/broadcast_in_dim | solution.py:543
  3.9 93.9 %shard_map.86 = (bf16[512,1024]{1,0:T(8,128)(2,1)}, f32[8,128]{1,0:T(8,128)}) custom-call(s32[4]{0:T(128)} %doc_ref.1, s32[16,8]{1,0:T(8,128)} %copy.9.table_ref, bf16[512,4096]{1,0:T(8,128)(2,1)} %hid_ref.1, bf16[1,4096]{1,0:T(2,128)(2,1)} %broadcast_in_dim.6.gain_ref, f32[1,128]{1,0:T(1,128)} %maximum_bitcast_fusion.freq_ref, bf16[1024,256]{1,0:T(8,128)(2,1)} %q_ref.1, ...), custom_call_target="tpu_custom_call" | custom-call | flops 4000000000 | bytes 8388608 | tf_op jit(solution)/shard_map/pallas_call | solution.py:491
  97.8 2.3 %copy.13 = bf16[512,1024]{1,0:T(8,128)(2,1)} copy(bf16[512,1024]{1,0:T(8,128)(2,1)} %get-tuple-element.10) | data formatting | bytes 2097152
  100.1 1.3 %copy.14 = f32[1,8,1,128]{3,2,1,0:T(1,128)} copy(f32[1,8,1,128]{3,2,1,0:T(1,128)} %bitcast.5) | data formatting | bytes 8192
  (1 shorter events, 0.0 us)

commit v5 on v1

--- a/solution.py
+++ b/solution.py
@@ -326,6 +326,19 @@
     diagonal = lax.broadcasted_iota(jnp.int32, (BLOCK, BLOCK), 0) == lax.broadcasted_iota(
         jnp.int32, (BLOCK, BLOCK), 1
     )
+    def forward(b):
+        for dx in range(1, heads):
+            source = lax.rem(x + dx, heads)
+            arrived(True, att.at[source * subs + c, b], a_recv.at[source, b])
+            send(
+                True,
+                att.at[source * subs + c, b],
+                att.at[source * subs + c, b],
+                ac_send.at[dx, b],
+                ac_recv.at[source, b],
+                (y, t, x, twin),
+            )
+
     for b in range(blocks):
         keys = window[0, b * BLOCK : b * BLOCK + reach, :]
         values = window[1, b * BLOCK : b * BLOCK + reach, :]
@@ -371,6 +384,8 @@
             ac_recv.at[x, b],
             (y, t, x, twin),
         )
+        if b:
+            forward(b - 1)
 
     me = t * subs + c
     for dt in range(toks):
@@ -392,30 +407,23 @@
             arrived(True, dst, o_recv.at[r, side])
     share_cols = out_ref.shape[1]
     columns = pl.ds(pl.multiple_of(mine * share_cols, share_cols), share_cols)
-    for b in range(blocks):
-        for dx in range(1, heads):
-            source = lax.rem(x + dx, heads)
-            arrived(True, att.at[source * subs + c, b], a_recv.at[source, b])
-            send(
-                True,
-                att.at[source * subs + c, b],
-                att.at[source * subs + c, b],
-                ac_send.at[dx, b],
-                ac_recv.at[source, b],
-                (y, t, x, twin),
-            )
-    for b in range(blocks):
-        for dx in range(heads):
-            source = lax.rem(x + dx, heads)
-            arrived(True, att.at[source * subs + twin, b], ac_recv.at[source, b])
-        at = slice(b * BLOCK, (b + 1) * BLOCK)
-        summed = jnp.zeros((BLOCK, share_cols), jnp.float32)
+    pair = 2
+    for first in range(0, blocks, pair):
+        if first + pair == blocks:
+            forward(blocks - 1)
+        for b in range(first, first + pair):
+            for dx in range(heads):
+                source = lax.rem(x + dx, heads)
+                arrived(True, att.at[source * subs + twin, b], ac_recv.at[source, b])
+        at = slice(first * BLOCK, (first + pair) * BLOCK)
+        summed = jnp.zeros((pair * BLOCK, share_cols), jnp.float32)
         for r in range(shares):
-            summed += (
-                jnp.dot(att[r, b], wo[r], preferred_element_type=jnp.float32)
-                .astype(jnp.bfloat16)
-                .astype(jnp.float32)
-            )
+            product = jnp.dot(
+                att[r, first : first + pair].reshape(pair * BLOCK, att.shape[3]),
+                wo[r],
+                preferred_element_type=jnp.float32,
+            )
+            summed += product.astype(jnp.bfloat16).astype(jnp.float32)
         out_ref[at, :] = (hid[at, columns].astype(jnp.float32) + summed).astype(jnp.bfloat16)
 
     group_heads = heads_here * subs

time: 84.1 us -> 88.2 us (1.049)
  the two profiles are of different devices: /device:TPU:6 before, /device:TPU:1 now
where the time goes in v5:
time: 88.2 us; the launch traced here: 87.9 us
  Pallas kernels  80.5 us (91%)
  local copies, waits for them, and re-layouts  6.19 us (7%)
    pallas_call x1, Pallas kernels, body(): pl.pallas_call(functools.partial(kernel, sizes), out_shape=(jax.ShapeDtyp...  80.5 us
    unnamed x3, local copies, waits for them, and re-layouts  4.88 us

profile of v5, /device:TPU:1, one launch (start us, length us, event | category | flops | bytes accessed | tf_op | source)
XLA Modules:
  0.0 87.9 jit_solution(233873339251105918)
XLA Ops:
  0.6 0.6 maximum_bitcast_fusion.freq_ref
  1.2 1.4 %copy.9.table_ref = s32[16,8]{1,0:T(8,128)} copy(s32[16,8]{0,1:T(8,128)} %param.13) | data formatting | bytes 1024 | tf_op args[6]
  2.6 1.3 %broadcast_in_dim.6.gain_ref = bf16[1,4096]{1,0:T(2,128)(2,1)} reshape(bf16[4096]{0:T(1024)(128)(2,1)} %param.8) | data formatting | bytes 16384 | tf_op jit(solution)/shard_map/broadcast_in_dim | solution.py:522
  3.9 80.5 %shard_map.86 = (bf16[512,1024]{1,0:T(8,128)(2,1)}, f32[8,128]{1,0:T(8,128)}) custom-call(s32[4]{0:T(128)} %doc_ref.1, s32[16,8]{1,0:T(8,128)} %copy.9.table_ref, bf16[512,4096]{1,0:T(8,128)(2,1)} %hid_ref.1, bf16[1,4096]{1,0:T(2,128)(2,1)} %broadcast_in_dim.6.gain_ref, f32[1,128]{1,0:T(1,128)} %maximum_bitcast_fusion.freq_ref, bf16[1024,256]{1,0:T(8,128)(2,1)} %q_ref.1, ...), custom_call_target="tpu_custom_call" | custom-call | flops 4000000000 | bytes 8388608 | tf_op jit(solution)/shard_map/pallas_call | solution.py:470
  84.4 2.3 %copy.13 = bf16[512,1024]{1,0:T(8,128)(2,1)} copy(bf16[512,1024]{1,0:T(8,128)(2,1)} %get-tuple-element.10) | data formatting | bytes 2097152
  86.6 1.3 %copy.14 = f32[1,8,1,128]{3,2,1,0:T(1,128)} copy(f32[1,8,1,128]{3,2,1,0:T(1,128)} %bitcast.5) | data formatting | bytes 8192
  (1 shorter events, 0.0 us)
